TPU v7x, 32 devices: a whole 2x2x4 slice. The times are simulated.
32 devices in a mesh: table: 2 (over x), image: 16 (over z, y, core).
Axes of the slice: x: 2, y: 2, z: 4, core: 2. Of those that a mesh axis runs over, the one named last changes fastest.
Arguments:
- traces: bfloat16 [512, 1920], P(('table', 'image')), may hold values from -6 to 6
- aperture: int32 [512, 4], P(('table', 'image')), may hold values from 0 to 15, all different within a row; in each aligned block of 16 rows (0 to 15, 16 to 31, ...) at most 8 rows name the same one
- bucket: int32 [512], P(('table', 'image')), may hold values from 0 to 3
- table_node: int32 [512, 4], P(('table', 'image')), may hold values from 0 to 15
- entry_gain: bfloat16 [512, 4], P(('table', 'image')), may hold values from 0.5 to 2
- travel: float32 [16, 16, 1024], P('image', None, 'table'), may hold values from 1 to 1918
- spread: float32 [16, 16, 1024], P('image', None, 'table'), may hold values from 0.1 to 1
Outputs:
- image: float32 [16, 1024], P('image', 'table')
Inputs may be any that keep to these rules, and one draw needn't show every extreme that they name: `aperture`: each trace names 4 different tiles. Among the 16 traces of one device at most 8 name the same tile, and in every draw some tile is named by exactly 8 of them.
All inputs are finite; a program needn't handle non-finite values.
Results may differ from a plain program's by a relative error of at most 0.0024.
Values may be sent and summed in bfloat16 or wider, within the bound.
A program may use at most 128 MiB of HBM per device.

v0:
```python
import math
import jax
import jax.numpy as jnp
from jax import lax
from jax.sharding import PartitionSpec as P

max_lag = 7


def antialias(trace_rows, filter_index):
    half_width = (2 + 2 * filter_index).astype(jnp.float32)[..., None]
    length = trace_rows.shape[-1]
    widths = [(0, 0)] * (trace_rows.ndim - 1) + [(max_lag, max_lag)]
    padded = jnp.pad(trace_rows, widths)
    summed = jnp.zeros(trace_rows.shape, jnp.float32)
    for sample_lag in range(-max_lag, max_lag + 1):
        ramp_weight = jnp.maximum(half_width - abs(sample_lag), 0.0) / (half_width * half_width)
        window = lax.slice_in_dim(
            padded, max_lag + sample_lag, max_lag + sample_lag + length, axis=trace_rows.ndim - 1
        )
        summed = summed + ramp_weight * window
    return summed


def interpolate(stack_tile, travel_tile, spread_tile):
    floor_value = jnp.floor(travel_tile)
    fraction = travel_tile - floor_value
    lower_index = floor_value.astype(jnp.int32)
    shifted = jnp.pad(stack_tile[:, 1:], ((0, 0), (0, 1)))
    paired = jnp.stack([stack_tile, shifted], axis=-1)
    picked = jnp.take_along_axis(paired, lower_index[:, :, None], axis=1)
    lower_value = picked[:, :, 0]
    upper_value = picked[:, :, 1]
    return jnp.sum(spread_tile * ((1.0 - fraction) * lower_value + fraction * upper_value), axis=0)


def per_device(traces, aperture, bucket, table_node, entry_gain, travel, spread):
    tiles = lax.axis_size("image")
    groups = lax.axis_size("table")
    trace_count, samples = traces.shape
    aper_count = aperture.shape[1]
    node_count = travel.shape[1]
    capacity = max(2, 2 * trace_count * aper_count // tiles)
    entries = trace_count * aper_count
    destination = aperture.reshape(entries)
    member = (destination[:, None] == jnp.arange(tiles, dtype=jnp.int32)[None, :]).astype(jnp.int32)
    earlier = jnp.cumsum(member, axis=0) - member
    slot_index = jnp.sum(earlier * member, axis=1)
    source_row = jnp.arange(entries, dtype=jnp.int32) // aper_count
    flat_nodes = table_node.reshape(entries)
    flat_gains = entry_gain.reshape(entries)
    node_slots = jnp.zeros((capacity, tiles), jnp.int32).at[slot_index, destination].set(flat_nodes)
    raw_slots = (
        jnp.zeros((capacity, tiles, samples), jnp.bfloat16)
        .at[slot_index, destination]
        .set(traces[source_row])
    )
    gain_slots = (
        jnp.zeros((capacity, tiles), jnp.bfloat16).at[slot_index, destination].set(flat_gains)
    )
    filter_slots = (
        jnp.zeros((capacity, tiles), jnp.int32).at[slot_index, destination].set(bucket[source_row])
    )
    raw_part = lax.all_to_all(raw_slots, "image", split_axis=1, concat_axis=1, tiled=True)
    gain_part = lax.all_to_all(gain_slots, "image", split_axis=1, concat_axis=1, tiled=True)
    filter_part = lax.all_to_all(filter_slots, "image", split_axis=1, concat_axis=1, tiled=True)
    node_part = lax.all_to_all(node_slots, "image", split_axis=1, concat_axis=1, tiled=True)
    filtered = antialias(raw_part.astype(jnp.float32), filter_part)
    weighted = (gain_part.astype(jnp.float32)[..., None] * filtered).astype(jnp.bfloat16)
    slot_total = tiles * capacity
    flat_values = weighted.reshape(slot_total, samples)
    node_member = (
        node_part.reshape(slot_total)[:, None] == jnp.arange(node_count, dtype=jnp.int32)[None, :]
    ).astype(jnp.bfloat16)
    stack = lax.dot_general(
        node_member, flat_values, (((0,), (0,)), ((), ())), preferred_element_type=jnp.float32
    )
    scale = 1.0 / math.sqrt(trace_count * groups * aper_count)
    summed_stack = lax.psum(stack, "table")
    return (interpolate(summed_stack, travel[0], spread[0]) * scale)[None, :]


def solution(mesh):
    in_specs = (
        P(("table", "image"), None),
        P(("table", "image"), None),
        P(("table", "image")),
        P(("table", "image"), None),
        P(("table", "image"), None),
        P("image", None, "table"),
        P("image", None, "table"),
    )
    out_specs = P("image", "table")
    return jax.shard_map(
        per_device, mesh=mesh, in_specs=in_specs, out_specs=out_specs, check_vma=False
    )
```

profile of v0, /device:TPU:0, one launch (start us, length us, event | category | flops | bytes accessed | tf_op | source)
XLA Modules:
  0.0 235.3 jit_solution(4942274203572084065)
XLA Ops:
  6.5 0.0 copy-start
  6.5 0.8 copy.41
  7.3 0.1 eq.30
  7.4 0.1 reshape.171
  7.5 0.1 fusion.22
  7.6 0.1 reduce_window_sum.11
  7.7 0.2 select_reduce_fusion
  7.8 0.8 copy.46
  8.6 0.1 reshape.206
  8.7 3.5 %scatter_fusion.1 = bf16[8,16]{1,0:T(8,128)(2,1)S(1)} fusion(bf16[8,16]{1,0:T(8,128)(2,1)S(1)} %broadcast_in_dim.11, s32[64]{0:T(128)S(1)} %fusion.25, bf16[64]{0:T(256)(128)(2,1)S(1)} %reshape.206), kind=kCustom, calls=%fused_computation.4 | custom fusion | bytes 896 | tf_op jit(solution)/shard_map/scatter | solution.py:59
  12.3 0.7 copy.47
  12.9 7.4 %all-to-all-start.1 = ((bf16[8,16,1]{0,2,1:T(2,128)(2,1)}), bf16[8,16,1]{0,2,1:T(2,128)(2,1)S(1)}, u32[]{:S(2)}, u32[]{:S(2)}) async-start(bf16[8,16,1]{0,2,1:T(2,128)(2,1)} %copy.47), calls=%async_computation.1 | async-start | bytes 16384 | tf_op jit(solution)/shard_map/all_to_all | solution.py:65
  20.4 1.4 gather_fusion
  21.8 3.5 %scatter_fusion.2 = s32[8,16]{1,0:T(8,128)S(1)} fusion(s32[8,16]{1,0:T(8,128)S(1)} %broadcast.222.clone, s32[64]{0:T(128)S(1)} %fusion.25, s32[64]{0:T(128)S(1)} %gather_fusion), kind=kCustom, calls=%fused_computation.5 | custom fusion | bytes 1280 | tf_op jit(solution)/shard_map/scatter | solution.py:62
  25.3 0.7 copy.49
  25.9 0.8 all-to-all-done.1
  26.7 5.2 %all-to-all-start.2 = ((s32[8,16,1]{0,2,1:T(1,128)}), s32[8,16,1]{0,2,1:T(1,128)S(1)}, u32[]{:S(2)}, u32[]{:S(2)}) async-start(s32[8,16,1]{0,2,1:T(1,128)} %copy.49), calls=%async_computation.2 | async-start | bytes 16384 | tf_op jit(solution)/shard_map/all_to_all | solution.py:66
  31.9 0.8 copy.43
  32.7 0.1 reshape.200
  32.8 3.5 %scatter_fusion = s32[8,16]{1,0:T(8,128)S(1)} fusion(s32[8,16]{1,0:T(8,128)S(1)} %broadcast.222.clone.1, s32[64]{0:T(128)S(1)} %fusion.25, s32[64]{0:T(128)S(1)} %reshape.200), kind=kCustom, calls=%fused_computation.3 | custom fusion | bytes 1280 | tf_op jit(solution)/shard_map/scatter | solution.py:52
  36.3 0.7 copy.44
  36.9 1.4 all-to-all-done.2
  38.4 4.6 %all-to-all-start = ((s32[8,16,1]{0,2,1:T(1,128)}), s32[8,16,1]{0,2,1:T(1,128)S(1)}, u32[]{:S(2)}, u32[]{:S(2)}) async-start(s32[8,16,1]{0,2,1:T(1,128)} %copy.44), calls=%async_computation | async-start | bytes 16384 | tf_op jit(solution)/shard_map/all_to_all | solution.py:67
  43.0 0.0 copy-done
  43.0 0.0 copy-start.1
  43.0 0.8 gather_fusion.1
  43.8 6.3 %scatter_fusion.3 = bf16[8,16,1920]{2,1,0:T(8,128)(2,1)S(1)} fusion(bf16[8,16,1920]{2,1,0:T(8,128)(2,1)S(1)} %broadcast_in_dim.12, s32[64]{0:T(128)S(1)} %fusion.25, bf16[64,1920]{1,0:T(8,128)(2,1)S(1)} %gather_fusion.1), kind=kCustom, calls=%fused_computation.6 | custom fusion | bytes 737792 | tf_op jit(solution)/shard_map/scatter | solution.py:56
  50.1 0.9 copy.51
  50.9 0.0 all-to-all-done
  50.9 6.0 %all-to-all-start.3 = ((bf16[8,16,1920]{2,0,1:T(8,128)(2,1)}), bf16[8,16,1920]{2,0,1:T(8,128)(2,1)S(1)}, u32[]{:S(2)}, u32[]{:S(2)}) async-start(bf16[8,16,1920]{2,0,1:T(8,128)(2,1)} %copy.51), calls=%async_computation.3 | async-start | bytes 983040 | tf_op jit(solution)/shard_map/all_to_all | solution.py:64
  56.9 0.0 all-reduce.4.cloned.1.call-start
  57.0 0.0 copy-done.1
  57.1 0.1 copy.48
  57.1 0.1 copy.45
  57.2 0.1 eq.34
  57.3 0.1 copy.50
  57.4 13.3 %all-to-all-done.3 = bf16[8,16,1920]{2,0,1:T(8,128)(2,1)S(1)} async-done(((bf16[8,16,1920]{2,0,1:T(8,128)(2,1)}), bf16[8,16,1920]{2,0,1:T(8,128)(2,1)S(1)}, u32[]{:S(2)}, u32[]{:S(2)}) %all-to-all-start.3) | async-done | bytes 491552 | tf_op jit(solution)/shard_map/all_to_all | solution.py:64
  70.7 0.1 copy_convert_fusion
  70.8 4.0 %multiply_convert_fusion = bf16[8,16,1920]{2,1,0:T(8,128)(2,1)S(1)} fusion(f32[8,16,1920]{2,1,0:T(8,128)S(1)} %copy_convert_fusion, f32[8,16]{1,0:T(8,128)S(1)} %get-tuple-element.6, f32[8,16]{1,0:T(8,128)S(1)} %get-tuple-element.7, f32[8,16]{1,0:T(8,128)S(1)} %get-tuple-element.8, f32[8,16]{1,0:T(8,128)S(1)} %get-tuple-element.9, ...), kind=kLoop, calls=%fused_computation.7 | loop fusion | flops 7618560 | bytes 1479168 | tf_op jit(solution)/shard_map/convert_element_type | solution.py:69
  74.8 0.9 fusion.11
  75.7 0.0 all-reduce.4.cloned.1.call-update
  75.8 20.8 %all-reduce.4.cloned.1.call-done = f32[16,1920]{1,0:T(8,128)} async-done(((f32[16,1920]{1,0:T(8,128)}), f32[16,1920]{1,0:T(8,128)}) %all-reduce.4.cloned.1.call-update) | async-done | bytes 122896 | tf_op jit(solution)/shard_map/psum | solution.py:79
  96.6 1.0 slice.83
  97.6 0.9 pad_maximum_fusion
  98.6 7.8 %copy.53 = f32[16,1920,2]{2,1,0:T(8,128)} copy(f32[16,1920,2]{1,0,2:T(8,128)S(1)} %pad_maximum_fusion) | data formatting | bytes 491520 | tf_op jit(solution)/shard_map/stack | solution.py:30
  106.3 118.6 %gather_fusion.2 = f32[8192,2]{1,0:T(8,128)} fusion(f32[16,1920,2]{2,1,0:T(8,128)} %copy.53, s32[8192]{0:T(1024)S(1)} %bitcast.70), kind=kCustom, calls=%fused_computation.2 | custom fusion | bytes 196608 | tf_op jit(solution)/shard_map/jit(take_along_axis)/gather | solution.py:31
  225.0 0.0 copy-start.2
  225.0 2.8 %copy.54 = f32[16,512,2]{1,0,2:T(8,128)S(1)} copy(f32[16,512,2]{2,1,0:T(8,128)} %bitcast.74) | data formatting | bytes 131072 | tf_op jit(solution)/shard_map/jit(take_along_axis)/gather | solution.py:31
  227.8 0.0 copy-done.2
  227.9 0.6 broadcast_multiply_fusion
  (15 shorter events, 0.2 us)
Async XLA Ops:
  6.5 36.4 %copy-start = (bf16[16,1920]{1,0:T(8,128)(2,1)S(1)}, bf16[16,1920]{1,0:T(8,128)(2,1)}, u32[]{:S(2)}) copy-start(bf16[16,1920]{1,0:T(8,128)(2,1)} %param.7) | copy-start | bytes 184324
  12.9 13.8 %all-to-all-start.1 = ((bf16[8,16,1]{0,2,1:T(2,128)(2,1)}), bf16[8,16,1]{0,2,1:T(2,128)(2,1)S(1)}, u32[]{:S(2)}, u32[]{:S(2)}) async-start(bf16[8,16,1]{0,2,1:T(2,128)(2,1)} %copy.47), calls=%async_computation.1 | async-start | bytes 16384 | tf_op jit(solution)/shard_map/all_to_all | solution.py:65
  26.7 11.6 %all-to-all-start.2 = ((s32[8,16,1]{0,2,1:T(1,128)}), s32[8,16,1]{0,2,1:T(1,128)S(1)}, u32[]{:S(2)}, u32[]{:S(2)}) async-start(s32[8,16,1]{0,2,1:T(1,128)} %copy.49), calls=%async_computation.2 | async-start | bytes 16384 | tf_op jit(solution)/shard_map/all_to_all | solution.py:66
  38.4 12.6 %all-to-all-start = ((s32[8,16,1]{0,2,1:T(1,128)}), s32[8,16,1]{0,2,1:T(1,128)S(1)}, u32[]{:S(2)}, u32[]{:S(2)}) async-start(s32[8,16,1]{0,2,1:T(1,128)} %copy.44), calls=%async_computation | async-start | bytes 16384 | tf_op jit(solution)/shard_map/all_to_all | solution.py:67
  43.0 14.0 %copy-start.1 = (f32[1,16,512]{2,1,0:T(8,128)S(1)}, f32[1,16,512]{2,1,0:T(8,128)}, u32[]{:S(2)}) copy-start(f32[1,16,512]{2,1,0:T(8,128)} %param.12) | copy-start | bytes 98308
  50.9 19.8 %all-to-all-start.3 = ((bf16[8,16,1920]{2,0,1:T(8,128)(2,1)}), bf16[8,16,1920]{2,0,1:T(8,128)(2,1)S(1)}, u32[]{:S(2)}, u32[]{:S(2)}) async-start(bf16[8,16,1920]{2,0,1:T(8,128)(2,1)} %copy.51), calls=%async_computation.3 | async-start | bytes 983040 | tf_op jit(solution)/shard_map/all_to_all | solution.py:64
  56.9 39.7 %all-reduce.4.cloned.1.call-start = ((), (), s32[]{:S(2)}) async-start(), calls=%async_computation.4 | async-start | bytes 245760 | tf_op jit(solution)/shard_map/psum | solution.py:79
  225.0 2.9 %copy-start.2 = (f32[1,16,512]{2,1,0:T(8,128)S(1)}, f32[1,16,512]{2,1,0:T(8,128)}, u32[]{:S(2)}) copy-start(f32[1,16,512]{2,1,0:T(8,128)} %param.13) | copy-start | bytes 98308
Sparse Core Ops, SparseCore 0:
  75.9 20.6 all-reduce.3
where the time goes:
time: 236 us; the launch traced here: 235 us
  local copies, waits for them, and re-layouts  155 us (66%)
  waiting for transfers between devices  36.4 us (15%)
  starting transfers between devices  23.2 us (10%)
  between operations  13.6 us (6%)
  other arithmetic  6.02 us (3%)
    gather x2, local copies, waits for them, and re-layouts, interpolate(): picked = jnp.take_along_axis(paired, lower_index[:, :, None], axis=1)  121 us
    psum x1, waiting for transfers between devices, per_device(): summed_stack = lax.psum(stack, 'table')  20.8 us
    all_to_all x1, waiting for transfers between devices, per_device(): lax.all_to_all(raw_slots, 'image', split_axis=1, concat_axis=1, tiled=True)  13.3 us
    another operation x2, local copies, waits for them, and re-layouts, interpolate(): paired = jnp.stack([stack_tile, shifted], axis=-1)  7.79 us
    all_to_all x1, starting transfers between devices, per_device(): lax.all_to_all(gain_slots, 'image', split_axis=1, concat_axis=1, tiled=True)  7.39 us
    scatter x2, local copies, waits for them, and re-layouts, per_device(): raw_slots = jnp.zeros((capacity, tiles, samples), jnp.bfloat16).at[slot_i...  7.14 us
    scatter x2, local copies, waits for them, and re-layouts, per_device(): jnp.zeros((capacity, tiles), jnp.int32).at[slot_index, destination]  6.91 us
    all_to_all x1, starting transfers between devices, per_device(): lax.all_to_all(raw_slots, 'image', split_axis=1, concat_axis=1, tiled=True)  6.01 us
  transfers between devices with their start and end apart: 5, of which 4 were waited for; matrix products, arithmetic and copies ran while one was open for 8% of the time, Pallas kernels for 0%

commit v1 on v0

--- a/solution.py
+++ b/solution.py
@@ -5,6 +5,12 @@
 from jax.sharding import PartitionSpec as P
 
 max_lag = 7
+
+
+def stacked_exchange(x, name, split, join):
+    parts = jnp.split(x, lax.axis_size(name), axis=split)
+    arrived = lax.all_to_all(jnp.stack(parts), name, 0, 0)
+    return jnp.concatenate(arrived, axis=join)
 
 
 def antialias(trace_rows, filter_index):
@@ -61,7 +67,7 @@
     filter_slots = (
         jnp.zeros((capacity, tiles), jnp.int32).at[slot_index, destination].set(bucket[source_row])
     )
-    raw_part = lax.all_to_all(raw_slots, "image", split_axis=1, concat_axis=1, tiled=True)
+    raw_part = stacked_exchange(raw_slots, "image", 1, 1)
     gain_part = lax.all_to_all(gain_slots, "image", split_axis=1, concat_axis=1, tiled=True)
     filter_part = lax.all_to_all(filter_slots, "image", split_axis=1, concat_axis=1, tiled=True)
     node_part = lax.all_to_all(node_slots, "image", split_axis=1, concat_axis=1, tiled=True)

time: 236 us -> 248 us (1.051)
  local copies, waits for them, and re-layouts: 155 us -> 164 us
  waiting for transfers between devices: 36.4 us -> 40.7 us
    unnamed x10 -> x29, local copies, waits for them, and re-layouts: 2.33 us -> 10.8 us
    all_to_all x1, waiting for transfers between devices: 0.01 us -> 5.79 us  [per_device(): lax.all_to_all(node_slots, 'image', split_axis=1, concat_axis=1, tiled=True)]
    scatter x2 -> x1, local copies, waits for them, and re-layouts: 7.14 us -> 6.29 us  [per_device(): raw_slots = jnp.zeros((capacity, tiles, samples), jnp.bfloat16).at[slot_i...]
  transfers between devices with their start and end apart: 5 -> 5, of which waited for: 4 -> 4; matrix products, arithmetic and copies ran while one was open for 8% -> 11% of each run, Pallas kernels for 0% -> 0%
where the time goes in v1:
time: 248 us; the launch traced here: 247 us
  local copies, waits for them, and re-layouts  164 us (66%)
  waiting for transfers between devices  40.7 us (16%)
  starting transfers between devices  21.5 us (9%)
  between operations  13.7 us (6%)
  other arithmetic  5.97 us (2%)
    gather x2, local copies, waits for them, and re-layouts, interpolate(): picked = jnp.take_along_axis(paired, lower_index[:, :, None], axis=1)  121 us
    psum x1, waiting for transfers between devices, per_device(): summed_stack = lax.psum(stack, 'table')  20.7 us
    all_to_all x1, waiting for transfers between devices, stacked_exchange(): arrived = lax.all_to_all(jnp.stack(parts), name, 0, 0)  12.7 us
    unnamed x29, local copies, waits for them, and re-layouts  10.8 us
    another operation x2, local copies, waits for them, and re-layouts, interpolate(): paired = jnp.stack([stack_tile, shifted], axis=-1)  7.79 us
    all_to_all x1, starting transfers between devices, per_device(): lax.all_to_all(gain_slots, 'image', split_axis=1, concat_axis=1, tiled=True)  7.39 us
    scatter x2, local copies, waits for them, and re-layouts, per_device(): jnp.zeros((capacity, tiles), jnp.int32).at[slot_index, destination]  6.91 us
    scatter x1, local copies, waits for them, and re-layouts, per_device(): raw_slots = jnp.zeros((capacity, tiles, samples), jnp.bfloat16).at[slot_i...  6.29 us
  transfers between devices with their start and end apart: 5, of which 4 were waited for; matrix products, arithmetic and copies ran while one was open for 11% of the time, Pallas kernels for 0%

profile of v1, /device:TPU:0, one launch (start us, length us, event | category | flops | bytes accessed | tf_op | source)
XLA Modules:
  0.0 247.0 jit_solution(9768770589402737494)
XLA Ops:
  6.5 0.8 copy.389
  7.3 0.1 eq.30
  7.4 0.1 reshape.175
  7.5 0.1 fusion.22
  7.6 0.1 reduce_window_sum.11
  7.7 0.2 select_reduce_fusion
  7.8 0.8 copy.394
  8.6 0.1 reshape.211
  8.7 3.5 %scatter_fusion.1 = bf16[8,16]{1,0:T(8,128)(2,1)S(1)} fusion(bf16[8,16]{1,0:T(8,128)(2,1)S(1)} %broadcast_in_dim.11, s32[64]{0:T(128)S(1)} %fusion.25, bf16[64]{0:T(256)(128)(2,1)S(1)} %reshape.211), kind=kCustom, calls=%fused_computation.4 | custom fusion | bytes 896 | tf_op jit(solution)/shard_map/scatter | solution.py:65
  12.3 0.7 copy.395
  13.0 7.4 %all-to-all-start.1 = ((bf16[8,16,1]{0,2,1:T(2,128)(2,1)}), bf16[8,16,1]{0,2,1:T(2,128)(2,1)S(1)}, u32[]{:S(2)}, u32[]{:S(2)}) async-start(bf16[8,16,1]{0,2,1:T(2,128)(2,1)} %copy.395), calls=%async_computation.1 | async-start | bytes 16384 | tf_op jit(solution)/shard_map/all_to_all | solution.py:71
  20.4 0.8 gather_fusion.1
  21.2 6.3 %scatter_fusion.3 = bf16[8,16,1920]{2,1,0:T(8,128)(2,1)S(1)} fusion(bf16[8,16,1920]{2,1,0:T(8,128)(2,1)S(1)} %broadcast_in_dim.12, s32[64]{0:T(128)S(1)} %fusion.25, bf16[64,1920]{1,0:T(8,128)(2,1)S(1)} %gather_fusion.1), kind=kCustom, calls=%fused_computation.6 | custom fusion | bytes 737792 | tf_op jit(solution)/shard_map/scatter | solution.py:62
  27.5 0.8 fusion.26
  28.3 0.6 constant_dynamic-update-slice_fusion.15
  28.9 0.6 constant_dynamic-update-slice_fusion.14
  29.5 0.6 constant_dynamic-update-slice_fusion.13
  30.1 0.6 constant_dynamic-update-slice_fusion.12
  30.8 0.6 constant_dynamic-update-slice_fusion.11
  31.4 0.6 constant_dynamic-update-slice_fusion.10
  32.0 0.6 constant_dynamic-update-slice_fusion.9
  32.6 0.6 constant_dynamic-update-slice_fusion.8
  33.2 0.6 constant_dynamic-update-slice_fusion.7
  33.8 0.6 constant_dynamic-update-slice_fusion.6
  34.4 0.6 constant_dynamic-update-slice_fusion.5
  35.1 0.6 constant_dynamic-update-slice_fusion.4
  35.7 0.6 constant_dynamic-update-slice_fusion.3
  36.3 0.6 constant_dynamic-update-slice_fusion.2
  36.9 0.8 gather_fusion
  37.7 3.5 %scatter_fusion.2 = s32[8,16]{1,0:T(8,128)S(1)} fusion(s32[8,16]{1,0:T(8,128)S(1)} %broadcast.222.clone, s32[64]{0:T(128)S(1)} %fusion.25, s32[64]{0:T(128)S(1)} %gather_fusion), kind=kCustom, calls=%fused_computation.5 | custom fusion | bytes 1280 | tf_op jit(solution)/shard_map/scatter | solution.py:68
  41.1 0.7 copy.398
  41.8 6.0 %all-to-all-start.2 = ((s32[8,16,1]{0,2,1:T(1,128)}), s32[8,16,1]{0,2,1:T(1,128)S(1)}, u32[]{:S(2)}, u32[]{:S(2)}) async-start(s32[8,16,1]{0,2,1:T(1,128)} %copy.398), calls=%async_computation.2 | async-start | bytes 16384 | tf_op jit(solution)/shard_map/all_to_all | solution.py:72
  47.8 0.6 constant_dynamic-update-slice_fusion.1
  48.4 0.1 copy.391
  48.5 0.1 reshape.205
  48.6 3.5 %scatter_fusion = s32[8,16]{1,0:T(8,128)S(1)} fusion(s32[8,16]{1,0:T(8,128)S(1)} %broadcast.222.clone.1, s32[64]{0:T(128)S(1)} %fusion.25, s32[64]{0:T(128)S(1)} %reshape.205), kind=kCustom, calls=%fused_computation.3 | custom fusion | bytes 1280 | tf_op jit(solution)/shard_map/scatter | solution.py:58
  52.1 0.7 copy.392
  52.7 1.5 all-to-all-done.2
  54.2 4.5 %all-to-all-start = ((s32[8,16,1]{0,2,1:T(1,128)}), s32[8,16,1]{0,2,1:T(1,128)S(1)}, u32[]{:S(2)}, u32[]{:S(2)}) async-start(s32[8,16,1]{0,2,1:T(1,128)} %copy.392), calls=%async_computation | async-start | bytes 16384 | tf_op jit(solution)/shard_map/all_to_all | solution.py:73
  58.8 0.6 constant_dynamic-update-slice_fusion
  59.4 5.8 %all-to-all-done = s32[8,16,1]{0,2,1:T(1,128)S(1)} async-done(((s32[8,16,1]{0,2,1:T(1,128)}), s32[8,16,1]{0,2,1:T(1,128)S(1)}, u32[]{:S(2)}, u32[]{:S(2)}) %all-to-all-start) | async-done | bytes 544 | tf_op jit(solution)/shard_map/all_to_all | solution.py:73
  65.2 3.6 %all-to-all-start.3 = ((bf16[16,8,1,1920]{3,1,2,0:T(8,128)(2,1)}), bf16[16,8,1,1920]{3,1,2,0:T(8,128)(2,1)S(1)}, u32[]{:S(2)}, u32[]{:S(2)}) async-start(bf16[16,8,1,1920]{3,1,2,0:T(8,128)(2,1)} %constant_dynamic-update-slice_fusion), calls=%async_computation.3 | async-start | bytes 983040 | tf_op jit(solution)/shard_map/all_to_all | solution.py:12
  68.8 0.1 copy.396
  68.9 0.1 copy.397
  69.0 0.1 copy.399
  69.1 0.1 copy.400
  69.2 0.1 copy.401
  69.2 0.1 copy.402
  69.3 0.1 copy.403
  69.4 0.1 copy.404
  69.5 0.1 copy.405
  69.5 0.1 copy.406
  69.6 0.1 copy.407
  69.7 0.1 eq.34
  69.8 12.7 %all-to-all-done.3 = bf16[16,8,1,1920]{3,1,2,0:T(8,128)(2,1)S(1)} async-done(((bf16[16,8,1,1920]{3,1,2,0:T(8,128)(2,1)}), bf16[16,8,1,1920]{3,1,2,0:T(8,128)(2,1)S(1)}, u32[]{:S(2)}, u32[]{:S(2)}) %all-to-all-start.3) | async-done | bytes 491552 | tf_op jit(solution)/shard_map/all_to_all | solution.py:12
  82.5 3.9 %multiply_convert_fusion = bf16[8,16,1920]{2,0,1:T(8,128)(2,1)S(1)} fusion(f32[8,16,1920]{2,0,1:T(8,128)S(1)} %convert_bitcast_fusion, f32[8,16]{0,1:T(8,128)S(1)} %copy.407, f32[8,16]{0,1:T(8,128)S(1)} %copy.406, f32[8,16]{0,1:T(8,128)S(1)} %copy.405, f32[8,16]{0,1:T(8,128)S(1)} %copy.404, f32[8,16]{0,1:T(8,128)S(1)} %copy.403, f32[8,16]{0,1:T(8,128)S(1)} %copy.402, ...), kind=kLoop, calls=%fused_computation.8 | loop fusion | flops 7618560 | bytes 1479168 | tf_op jit(solution)/shard_map/convert_element_type | solution.py:75
  86.5 0.9 fusion.11
  87.5 20.7 %all-reduce.4.cloned.1.call-done = f32[16,1920]{1,0:T(8,128)} async-done(((f32[16,1920]{1,0:T(8,128)}), f32[16,1920]{1,0:T(8,128)}) %all-reduce.4.cloned.1.call-update) | async-done | bytes 122896 | tf_op jit(solution)/shard_map/psum | solution.py:85
  108.3 1.0 slice.83
  109.3 0.9 pad_maximum_fusion
  110.2 7.8 %copy.409 = f32[16,1920,2]{2,1,0:T(8,128)} copy(f32[16,1920,2]{1,0,2:T(8,128)S(1)} %pad_maximum_fusion) | data formatting | bytes 491520 | tf_op jit(solution)/shard_map/stack | solution.py:36
  118.0 118.6 %gather_fusion.2 = f32[8192,2]{1,0:T(8,128)} fusion(f32[16,1920,2]{2,1,0:T(8,128)} %copy.409, s32[8192]{0:T(1024)S(1)} %bitcast.106), kind=kCustom, calls=%fused_computation.2 | custom fusion | bytes 196608 | tf_op jit(solution)/shard_map/jit(take_along_axis)/gather | solution.py:37
  236.6 2.8 %copy.410 = f32[16,512,2]{1,0,2:T(8,128)S(1)} copy(f32[16,512,2]{2,1,0:T(8,128)} %bitcast.110) | data formatting | bytes 131072 | tf_op jit(solution)/shard_map/jit(take_along_axis)/gather | solution.py:37
  239.5 0.6 broadcast_multiply_fusion
  (31 shorter events, 0.5 us)
Async XLA Ops:
  6.5 13.8 %copy-start = (bf16[16,1920]{1,0:T(8,128)(2,1)S(1)}, bf16[16,1920]{1,0:T(8,128)(2,1)}, u32[]{:S(2)}) copy-start(bf16[16,1920]{1,0:T(8,128)(2,1)} %param.7) | copy-start | bytes 184324
  13.0 28.9 %all-to-all-start.1 = ((bf16[8,16,1]{0,2,1:T(2,128)(2,1)}), bf16[8,16,1]{0,2,1:T(2,128)(2,1)S(1)}, u32[]{:S(2)}, u32[]{:S(2)}) async-start(bf16[8,16,1]{0,2,1:T(2,128)(2,1)} %copy.395), calls=%async_computation.1 | async-start | bytes 16384 | tf_op jit(solution)/shard_map/all_to_all | solution.py:71
  21.1 15.8 %copy-start.1 = (s32[16]{0:T(128)S(1)}, s32[16]{0:T(128)}, u32[]{:S(2)}) copy-start(s32[16]{0:T(128)} %param.9) | copy-start | bytes 196
  21.2 27.2 %copy-start.4 = (s32[16,4]{0,1:T(4,128)S(1)}, s32[16,4]{0,1:T(4,128)}, u32[]{:S(2)}) copy-start(s32[16,4]{0,1:T(4,128)} %param.10) | copy-start | bytes 772
  27.5 41.3 %copy-start.2 = (f32[1,16,512]{2,1,0:T(8,128)S(1)}, f32[1,16,512]{2,1,0:T(8,128)}, u32[]{:S(2)}) copy-start(f32[1,16,512]{2,1,0:T(8,128)} %param.12) | copy-start | bytes 98308
  41.8 12.4 %all-to-all-start.2 = ((s32[8,16,1]{0,2,1:T(1,128)}), s32[8,16,1]{0,2,1:T(1,128)S(1)}, u32[]{:S(2)}, u32[]{:S(2)}) async-start(s32[8,16,1]{0,2,1:T(1,128)} %copy.398), calls=%async_computation.2 | async-start | bytes 16384 | tf_op jit(solution)/shard_map/all_to_all | solution.py:72
  54.2 10.9 %all-to-all-start = ((s32[8,16,1]{0,2,1:T(1,128)}), s32[8,16,1]{0,2,1:T(1,128)S(1)}, u32[]{:S(2)}, u32[]{:S(2)}) async-start(s32[8,16,1]{0,2,1:T(1,128)} %copy.392), calls=%async_computation | async-start | bytes 16384 | tf_op jit(solution)/shard_map/all_to_all | solution.py:73
  65.2 17.3 %all-to-all-start.3 = ((bf16[16,8,1,1920]{3,1,2,0:T(8,128)(2,1)}), bf16[16,8,1,1920]{3,1,2,0:T(8,128)(2,1)S(1)}, u32[]{:S(2)}, u32[]{:S(2)}) async-start(bf16[16,8,1,1920]{3,1,2,0:T(8,128)(2,1)} %constant_dynamic-update-slice_fusion), calls=%async_computation.3 | async-start | bytes 983040 | tf_op jit(solution)/shard_map/all_to_all | solution.py:12
  68.7 39.5 %all-reduce.4.cloned.1.call-start = ((), (), s32[]{:S(2)}) async-start(), calls=%async_computation.4 | async-start | bytes 245760 | tf_op jit(solution)/shard_map/psum | solution.py:85
  236.6 2.9 %copy-start.3 = (f32[1,16,512]{2,1,0:T(8,128)S(1)}, f32[1,16,512]{2,1,0:T(8,128)}, u32[]{:S(2)}) copy-start(f32[1,16,512]{2,1,0:T(8,128)} %param.13) | copy-start | bytes 98308
Sparse Core Ops, SparseCore 0:
  87.6 20.6 all-reduce.3
